TPU v7x, 32 devices: a whole 2x2x4 slice. The times are simulated.
32 devices in a mesh: group: 2 (over x), patch: 16 (over z, y, core).
Axes of the slice: x: 2, y: 2, z: 4, core: 2. Of those that a mesh axis runs over, the one named last changes fastest.
Arguments:
- img_hidden: bfloat16 [2304, 3072], P(('group', 'patch')), parts along dimension 0, may hold values from -6 to 6
- img_qkv: bfloat16 [2304, 4608], P(('group', 'patch')), parts along dimension 0, may hold values from -6 to 6
- stale_kv: bfloat16 [2, 2304, 1536], P(None, ('group', 'patch')), parts along dimension 1, may hold values from -68 to 68
- txt_hidden: bfloat16 [64, 3072], P('group', 'patch'), parts along dimension 0, may hold values from -6 to 6
- txt_qkv: bfloat16 [64, 4608], P('group'), parts along dimension 0, may hold values from -6 to 6
- txt_mask: int32 [64], P('group'), parts along dimension 0, may hold values 0 or 1
- img_qk_gain: float32 [2, 128], replicated, may hold values from 0.1 to 1.9
- txt_qk_gain: float32 [2, 128], replicated, may hold values from 0.1 to 1.9
- img_gate: float32 [6144], P('group'), parts along dimension 0, may hold values from -4 to 4
- txt_gate: float32 [6144], P(('group', 'patch')), parts along dimension 0, may hold values from -4 to 4
- img_out_w: bfloat16 [1536, 3072], replicated, may hold values from -0.15625 to 0.15625
- txt_out_w: bfloat16 [1536, 3072], P(None, 'patch'), may hold values from -0.15625 to 0.15625
Outputs:
- img_out: bfloat16 [2304, 3072], P(('group', 'patch')), parts along dimension 0
- txt_out: bfloat16 [64, 3072], P('group', 'patch'), parts along dimension 0
- fresh_kv: bfloat16 [2, 2304, 1536], P(None, ('group', 'patch')), parts along dimension 1
There are 2 independent parts, one for each index of `group`. A program takes and returns all parts, laid end to end along the dimension named above; an argument that names none is the same for every part. Nothing has to cross between parts.
All inputs are finite; a program needn't handle non-finite values.
Results may differ from a plain program's by a relative error of at most 0.011.
Values may be sent and summed in bfloat16 or wider, within the bound.
A program may use at most 256 MiB of HBM per device.

v0:
```python
import math

import jax
import jax.numpy as jnp
from jax import lax
from jax.sharding import PartitionSpec as P

HEADS = 12
HD = 128


def merged(x, axis, combine):
    everything = jax.tree.map(
        lambda part, kind: lax.all_gather(part.astype(kind), axis),
        x,
        jax.tree.map(lambda a: jnp.bfloat16 if a.dtype == jnp.float32 else a.dtype, x),
    )

    def take(k):
        return jax.tree.map(lambda part, own: part[k].astype(own.dtype), everything, x)

    return lax.fori_loop(
        1, lax.axis_size(axis), lambda k, so_far: combine(so_far, take(k)), take(0)
    )


def head_norm(block, gain):
    lead = block.shape[0]
    split = block.reshape(lead, HEADS, HD)
    scaled = split * lax.rsqrt(jnp.mean(split * split, axis=-1, keepdims=True) + 1e-06) * gain
    return scaled.reshape(lead, HEADS * HD)


def prepare(qkv, gains):
    width = HEADS * HD
    raw = qkv.astype(jnp.float32)
    query = head_norm(raw[:, :width], gains[0]).astype(jnp.bfloat16)
    keys = head_norm(raw[:, width : 2 * width], gains[1]).astype(jnp.bfloat16)
    values = qkv[:, 2 * width :]
    return (query, keys, values)


def empty_state(rows):
    return (
        jnp.full((rows, HEADS), -1e30, jnp.float32),
        jnp.zeros((rows, HEADS), jnp.float32),
        jnp.zeros((rows, HEADS, HD), jnp.float32),
    )


def absorb(state, query_three, keys, values, valid):
    count = keys.shape[0]
    k_three = keys.reshape(count, HEADS, HD)
    v_three = values.reshape(count, HEADS, HD)
    scores = jnp.einsum(
        "rhd,khd->rhk", query_three, k_three, preferred_element_type=jnp.float32
    ) * (1.0 / math.sqrt(HD))
    scores = jnp.where(valid[None, None, :], scores, -jnp.inf)
    old_top, old_total, old_mixed = state
    new_top = jnp.maximum(old_top, jnp.max(scores, axis=-1))
    factor = jnp.exp(old_top - new_top)
    weights = jnp.exp(scores - new_top[..., None])
    new_total = old_total * factor + jnp.sum(weights, axis=-1)
    added = jnp.einsum(
        "rhk,khd->rhd", weights.astype(jnp.bfloat16), v_three, preferred_element_type=jnp.float32
    )
    return (new_top, new_total, old_mixed * factor[..., None] + added)


def join(first, second):
    top = jnp.maximum(first[0], second[0])
    left = jnp.exp(first[0] - top)
    right = jnp.exp(second[0] - top)
    return (
        top,
        first[1] * left + second[1] * right,
        first[2] * left[..., None] + second[2] * right[..., None],
    )


def finish(state):
    rows = state[2].shape[0]
    return (state[2] / state[1][..., None]).astype(jnp.bfloat16).reshape(rows, HEADS * HD)


def body(
    img_hidden,
    img_qkv,
    stale_kv,
    txt_hidden,
    txt_qkv,
    txt_mask,
    img_qk_gain,
    txt_qk_gain,
    img_gate,
    txt_gate,
    img_out_w,
    txt_out_w,
):
    rows = img_qkv.shape[0]
    text_rows = txt_qkv.shape[0]
    img_q, img_k, img_v = prepare(img_qkv, img_qk_gain)
    txt_q, txt_k, txt_v = prepare(txt_qkv, txt_qk_gain)
    fresh_kv = jnp.stack([img_k, img_v])
    query_three = img_q.reshape(rows, HEADS, HD)
    txt_valid = txt_mask == 1
    every_row = jnp.ones((rows,), dtype=bool)
    own_start = lax.axis_index("patch") * rows
    local = absorb(
        absorb(empty_state(rows), query_three, txt_k, txt_v, txt_valid),
        query_three,
        img_k,
        img_v,
        every_row,
    )
    piece = lax.all_gather(stale_kv, "patch", axis=1, tiled=True)
    count = piece.shape[1]
    place = jnp.arange(count, dtype=jnp.int32)
    valid = (place < own_start) | (place >= own_start + rows)
    state = absorb(local, query_three, piece[0], piece[1], valid)
    img_attn = finish(state)
    img_out = (
        img_hidden.astype(jnp.float32)
        + img_gate * jnp.dot(img_attn, img_out_w, preferred_element_type=jnp.float32)
    ).astype(jnp.bfloat16)
    text_three = txt_q.reshape(text_rows, HEADS, HD)
    partial_text = absorb(empty_state(text_rows), text_three, img_k, img_v, every_row)
    combined = merged(partial_text, "patch", join)
    combined = absorb(combined, text_three, txt_k, txt_v, txt_valid)
    txt_attn = finish(combined)
    txt_out = (
        txt_hidden.astype(jnp.float32)
        + txt_gate * jnp.dot(txt_attn, txt_out_w, preferred_element_type=jnp.float32)
    ).astype(jnp.bfloat16)
    return (img_out, txt_out, fresh_kv)


def solution(mesh):
    placed = (
        P(("group", "patch"), None),
        P(("group", "patch"), None),
        P(None, ("group", "patch"), None),
        P("group", "patch"),
        P("group", None),
        P("group"),
        P(),
        P(),
        P("group"),
        P(("group", "patch")),
        P(),
        P(None, "patch"),
    )
    return jax.shard_map(
        body,
        mesh=mesh,
        in_specs=placed,
        out_specs=(
            P(("group", "patch"), None),
            P("group", "patch"),
            P(None, ("group", "patch"), None),
        ),
        check_vma=False,
    )
```

profile of v0, /device:TPU:0, one launch (start us, length us, event | category | flops | bytes accessed | tf_op | source)
XLA Modules:
  0.0 200.0 jit_solution(186895771498463904)
XLA Ops:
  7.2 1.3 convert_element_type.137
  8.5 1.7 slice_bitcast_fusion
  11.0 1.1 mul.321
  16.2 2.1 %copy.65 = bf16[2,72,1536]{2,0,1:T(2,128)(2,1)} copy(bf16[2,72,1536]{2,1,0:T(8,128)(2,1)} %param.16) | data formatting | bytes 884736 | tf_op args[2]
  18.4 23.3 %all-gather.3 = bf16[16,32,12]{1,2,0:T(8,128)(2,1)S(1)} all-gather(bf16[1,32,12]{1,2,0:T(8,128)(2,1)S(1)} %convert_bitcast_fusion), channel_id=2, replica_groups=mesh['group'=2,'patch'=16] {'patch'}, dimensions={0}, use_global_device_ids=true | all-gather | bytes 13056 | tf_op jit(solution)/shard_map/all_gather | solution.py:14
  41.6 17.7 %all-gather.4 = bf16[16,32,12]{1,2,0:T(8,128)(2,1)S(1)} all-gather(bf16[1,32,12]{1,2,0:T(8,128)(2,1)S(1)} %get-tuple-element.243), channel_id=3, replica_groups=mesh['group'=2,'patch'=16] {'patch'}, dimensions={0}, use_global_device_ids=true | all-gather | bytes 13056 | tf_op jit(solution)/shard_map/all_gather | solution.py:14
  61.0 0.9 slice_convert_fusion
  62.0 21.2 %while.19 = (s32[]{:T(128)}, f32[32,12]{0,1:T(8,128)S(1)}, f32[32,12]{0,1:T(8,128)S(1)}, f32[32,12,128]{2,1,0:T(8,128)S(1)}, bf16[16,32,12]{1,2,0:T(8,128)(2,1)S...) while((s32[]{:T(128)}, f32[32,12]{0,1:T(8,128)S(1)}, ...), condition=%wide.region_13.14_spmd, body=%wide.region_12.13_spmd.sunk | while | flops 199685 | bytes 708247 | solution.py:22
  62.1 0.9 constant_dynamic-slice_fusion.2
  63.5 0.9 constant_dynamic-slice_fusion.2
  67.7 0.9 constant_dynamic-slice_fusion.2
  69.1 0.9 constant_dynamic-slice_fusion.2
  77.6 0.9 constant_dynamic-slice_fusion.2
  79.1 0.9 constant_dynamic-slice_fusion.2
  80.5 0.9 constant_dynamic-slice_fusion.2
  81.9 0.9 constant_dynamic-slice_fusion.2
  84.6 42.5 %all-gather.8.cloned.1.call-done = bf16[2,1152,1536]{2,0,1:T(2,128)(2,1)} async-done(((bf16[2,72,1536]{2,0,1:T(2,128)(2,1)}), bf16[2,1152,1536]{2,0,1:T(2,128)(2,1)}) %all-gather.8.cloned.1.call-update) | async-done | bytes 7077904 | tf_op jit(solution)/shard_map/all_gather | solution.py:116
  127.1 15.1 %fusion.110 = (bf16[1,1152,1536]{2,0,1:T(2,128)(2,1)}, bf16[1,1152,1536]{2,0,1:T(2,128)(2,1)}) fusion(bf16[2,1152,1536]{2,0,1:T(2,128)(2,1)} %all-gather.8.cloned.1.call-done), kind=kLoop, calls=%fused_computation.159 | loop fusion | bytes 14155776 | tf_op jit(solution)/shard_map/slice | solution.py:120
  142.2 15.9 %copy.88 = bf16[1,1152,1536]{1,2,0:T(8,128)(2,1)} copy(bf16[1,1152,1536]{2,0,1:T(2,128)(2,1)} %get-tuple-element.231) | data formatting | bytes 7077888
  158.1 4.7 %bitcast_reduce_fusion = (f32[72,12]{0,1:T(8,128)S(1)}, f32[12,72,1152]{2,1,0:T(8,128)}) fusion(bf16[1152,12,128]{0,2,1:T(8,128)(2,1)} %bitcast.240, bf16[9,12,8,128]{3,2,1,0:T(8,128)(2,1)S(1)} %get-tuple-element.232, pred[1152]{0:T(1024)(128)(4,1)S(1)} %fusion.102), kind=kOutput, calls=%fused_computation.13 | convolution fusion | flops 257789088 | bytes 7746048 | tf_op jit(solution)/shard_map/rhd,khd->rhk/dot_general | solution.py:55
  163.2 15.9 %copy.89 = bf16[1,1152,1536]{1,2,0:T(8,128)(2,1)} copy(bf16[1,1152,1536]{2,0,1:T(2,128)(2,1)} %get-tuple-element.230) | data formatting | bytes 7077888
  179.2 3.0 %fusion.6 = f32[72,12]{0,1:T(8,128)S(1)} fusion(f32[12,72,1152]{2,1,0:T(8,128)} %get-tuple-element.251, f32[72,12]{0,1:T(8,128)S(1)} %get-tuple-element.228), kind=kLoop, calls=%fused_computation.17 | loop fusion | flops 1989792 | bytes 3988224 | tf_op jit(solution)/shard_map/reduce_sum | solution.py:63
  183.0 3.9 %fusion.29 = bf16[12,9,8,128]{3,2,1,0:T(8,128)(2,1)S(1)} fusion(f32[72,12,128]{2,0,1:T(8,128)S(1)} %fusion.21, bf16[1152,12,128]{0,2,1:T(8,128)(2,1)} %bitcast.239, f32[12,72,1152]{2,1,0:T(8,128)S(1)} %copy-done.1, f32[72,12]{0,1:T(8,128)S(1)} %get-tuple-element.228, f32[72,12]{0,1:T(8,128)S(1)} %get-tuple-element.225), kind=kOutput, calls=%fused_computation.34 | convolution fusion | flops 257126400 | bytes 8190720 | tf_op jit(solution)/shard_map/rhk,khd->rhd/dot_general | solution.py:64
  186.9 6.2 %fusion.8 = bf16[72,3072]{1,0:T(8,128)(2,1)} fusion(bf16[1536,3072]{1,0:T(8,128)(2,1)} %param.24, bf16[72,3072]{1,0:T(8,128)(2,1)S(1)} %copy-done.5, f32[3072]{0:T(1024)S(1)} %copy-done.7, bf16[12,9,8,128]{3,2,1,0:T(8,128)(2,1)S(1)} %fusion.29), kind=kOutput, calls=%fused_computation.19 | convolution fusion | flops 680361984 | bytes 10555392 | tf_op jit(solution)/shard_map/dot_general | solution.py:124
  (146 shorter events, 22.3 us)
Async XLA Ops:
  7.2 76.5 %copy-start = (bf16[1536,192]{0,1:T(8,128)(2,1)S(1)}, bf16[1536,192]{0,1:T(8,128)(2,1)}, u32[]{:S(2)}) copy-start(bf16[1536,192]{0,1:T(8,128)(2,1)} %param.25) | copy-start | bytes 1769476
  7.2 5.2 %copy-start.9 = (f32[2,128]{1,0:T(2,128)S(1)}, f32[2,128]{1,0:T(2,128)}, u32[]{:S(2)}) copy-start(f32[2,128]{1,0:T(2,128)} %param.20) | copy-start | bytes 3076
  7.2 5.6 %copy-start.3 = (bf16[32,4608]{1,0:T(8,128)(2,1)S(1)}, bf16[32,4608]{1,0:T(8,128)(2,1)}, u32[]{:S(2)}) copy-start(bf16[32,4608]{1,0:T(8,128)(2,1)} %param.18) | copy-start | bytes 884740
  7.2 53.8 %all-gather.10.cloned.1.call-start = ((), (), s32[]{:S(2)}) async-start(), calls=%async_computation.1 | async-start | bytes 1671168 | tf_op jit(solution)/shard_map/all_gather | solution.py:14
  10.2 2.9 %copy-start.10 = (f32[2,128]{1,0:T(2,128)S(1)}, f32[2,128]{1,0:T(2,128)}, u32[]{:S(2)}) copy-start(f32[2,128]{1,0:T(2,128)} %param.21) | copy-start | bytes 3076
  13.5 45.8 %copy-start.11 = (s32[32]{0:T(128)S(1)}, s32[32]{0:T(128)}, u32[]{:S(2)}) copy-start(s32[32]{0:T(128)} %param.19) | copy-start | bytes 388
  13.7 46.1 %copy-start.2 = (bf16[1,72,1536]{2,1,0:T(8,128)(2,1)S(1)}, bf16[1,72,1536]{2,1,0:T(8,128)(2,1)}, u32[]{:S(2)}) copy-start(bf16[1,72,1536]{2,1,0:T(8,128)(2,1)} %get-tuple-element.236) | copy-start | bytes 663556
  16.1 110.9 %all-gather.8.cloned.1.call-start = ((), (), s32[]{:S(2)}) async-start(), calls=%async_computation | async-start | bytes 7520256 | tf_op jit(solution)/shard_map/all_gather | solution.py:116
  59.8 23.5 %copy-start.4 = (bf16[32,4608]{1,0:T(8,128)(2,1)S(1)}, bf16[32,4608]{1,0:T(8,128)(2,1)}, u32[]{:S(2)}) copy-start(bf16[32,4608]{1,0:T(8,128)(2,1)} %param.18) | copy-start | bytes 884740
  60.7 23.0 %copy-start.6 = (bf16[32,192]{1,0:T(8,128)(2,1)S(1)}, bf16[32,192]{1,0:T(8,128)(2,1)}, u32[]{:S(2)}) copy-start(bf16[32,192]{1,0:T(8,128)(2,1)} %param.17) | copy-start | bytes 36868
  60.7 23.0 %copy-start.8 = (f32[192]{0:T(256)S(1)}, f32[192]{0:T(256)}, u32[]{:S(2)}) copy-start(f32[192]{0:T(256)} %param.23) | copy-start | bytes 2308
  179.2 3.8 %copy-start.1 = (f32[12,72,1152]{2,1,0:T(8,128)S(1)}, f32[12,72,1152]{2,1,0:T(8,128)}, u32[]{:S(2)}) copy-start(f32[12,72,1152]{2,1,0:T(8,128)} %get-tuple-element.251) | copy-start | bytes 11943940
  183.0 3.9 %copy-start.5 = (bf16[72,3072]{1,0:T(8,128)(2,1)S(1)}, bf16[72,3072]{1,0:T(8,128)(2,1)}, u32[]{:S(2)}) copy-start(bf16[72,3072]{1,0:T(8,128)(2,1)} %param.14) | copy-start | bytes 1327108
  183.0 3.9 %copy-start.7 = (f32[3072]{0:T(1024)S(1)}, f32[3072]{0:T(1024)}, u32[]{:S(2)}) copy-start(f32[3072]{0:T(1024)} %param.22) | copy-start | bytes 36868
Sparse Core Ops, SparseCore 0:
  16.3 42.1 all-gather.9
  61.3 65.7 all-gather.7
where the time goes:
time: 202 us; the launch traced here: 200 us
  local copies, waits for them, and re-layouts  69.1 us (34%)
  waiting for transfers between devices  42.6 us (21%)
  blocking collectives  41 us (20%)
  matrix products  18.9 us (9%)
  between operations  14.5 us (7%)
  other arithmetic  13.3 us (7%)
    all_gather x1, waiting for transfers between devices, body(): piece = lax.all_gather(stale_kv, 'patch', axis=1, tiled=True)  42.5 us
    all_gather x2, blocking collectives, merged(): lax.all_gather(part.astype(kind), axis)  41 us
    unnamed x27, local copies, waits for them, and re-layouts  34 us
    slice x1, local copies, waits for them, and re-layouts, body(): state = absorb(local, query_three, piece[0], piece[1], valid)  15.1 us
    dynamic_slice x15, local copies, waits for them, and re-layouts, take(): part[k].astype(own.dtype)  13.7 us
    dot_general x1, matrix products, body(): jnp.dot(img_attn, img_out_w, preferred_element_type=jnp.float32)  6.24 us
    dot_general x5, matrix products, absorb(): jnp.einsum('rhk,khd->rhd', weights.astype(jnp.bfloat16), v_three, preferr...  6.06 us
    dot_general x5, matrix products, absorb(): jnp.einsum('rhd,khd->rhk', query_three, k_three, preferred_element_type=j...  5.69 us
  transfers between devices with their start and end apart: 2, of which 1 were waited for; matrix products, arithmetic and copies ran while one was open for 13% of the time, Pallas kernels for 0%

commit v1 on v0

v1 whole, which is shorter than its diff:
```python
import functools
import math

import jax
import jax.numpy as jnp
from jax import lax
from jax.experimental import pallas as pl
from jax.experimental.pallas import tpu as pltpu
from jax.sharding import PartitionSpec as P

HEADS = 12
HD = 128
GROUPS = 4
PER = HEADS // GROUPS
GW = PER * HD
HW = HEADS * HD
LOC = 128
LOW = -1e30
SCALE = 1.0 / math.sqrt(HD)
LOG2E = 1.0 / math.log(2.0)
F32 = jnp.float32
BF16 = jnp.bfloat16


def nt(x, y):
    return lax.dot_general(x, y, (((1,), (1,)), ((), ())), preferred_element_type=F32)


def lanes_of(rows):
    return lax.broadcasted_iota(jnp.int32, (rows, HD), 1)


def normed(x, gain):
    x = x.astype(F32)
    return (x * lax.rsqrt(jnp.mean(x * x, axis=-1, keepdims=True) + 1e-06) * gain).astype(BF16)


def soft(scores, values):
    top = jnp.max(scores, axis=-1, keepdims=True)
    weights = jnp.exp2((scores - top) * (SCALE * LOG2E))
    total = jnp.sum(weights, axis=-1, keepdims=True)
    mixed = jnp.dot(weights.astype(BF16), values, preferred_element_type=F32)
    return mixed / total, top * SCALE + jnp.log(total)


def pack(logs, rows):
    lane = lanes_of(rows)
    out = jnp.zeros((rows, HD), F32)
    for j, log in enumerate(logs):
        high = log.astype(BF16).astype(F32)
        rest = log - high
        mid = rest.astype(BF16).astype(F32)
        for i, part in enumerate((high, mid, rest - mid)):
            out = jnp.where(lane == 3 * j + i, part, out)
    return out.astype(BF16)


def unpack(block, j, rows):
    lane = lanes_of(rows)
    stats = block[:, GW : GW + HD].astype(F32)
    return jnp.sum(
        jnp.where((lane >= 3 * j) & (lane < 3 * j + 3), stats, 0.0), axis=-1, keepdims=True
    )


def merge(parts):
    top = functools.reduce(jnp.maximum, [log for _, log in parts])
    shares = [jnp.exp(log - top) for _, log in parts]
    total = functools.reduce(jnp.add, shares)
    mixed = functools.reduce(jnp.add, [share * part for share, (part, _) in zip(shares, parts)])
    return mixed / total, top + jnp.log(total)


def kernel(
    n,
    img_hidden,
    img_qkv,
    stale,
    txt_hidden,
    txt_qkv,
    txt_mask,
    img_gain,
    txt_gain,
    img_gate,
    txt_gate,
    w_hbm,
    txt_w,
    img_out,
    txt_out,
    fresh,
    kvbuf,
    qsend,
    qrecv,
    kfull,
    vfull,
    kloc,
    vloc,
    oloc,
    lloc,
    osend,
    orecv,
    tsend,
    tz,
    tpl,
    tfin,
    wbuf,
    acc,
    w_sem,
    kv_recv,
    a2a_send,
    sib_send,
    row_send,
    q_send,
    q_recv,
    o_send,
    o_recv,
    tz_send,
    tz_recv,
    tp_send,
    tp_recv,
    tf_send,
    tf_recv,
):
    A = GROUPS
    B = n // A
    rows = img_qkv.shape[0]
    trows = txt_qkv.shape[0]
    me = lax.axis_index("patch")
    a = me // B
    b = lax.rem(me, B)
    core = lax.rem(b, 2)
    sib = b + 1 - 2 * core
    chip = b // 2
    chips = B // 2

    def over(k):
        return lax.rem(a + k, A)

    def row_peer(j):
        return 2 * lax.rem(chip + j, chips) + core

    def remote(src, dst, send, recv, to_a, to_b):
        return pltpu.make_async_remote_copy(
            src_ref=src,
            dst_ref=dst,
            send_sem=send,
            recv_sem=recv,
            device_id={"patch": to_a * B + to_b},
            device_id_type=pl.DeviceIdType.MESH,
        )

    def got(dst, sem):
        remote(dst, dst, sem, sem, a, sib).wait_recv()

    started = []

    def go(copy):
        copy.start()
        started.append(copy)

    load_w = pltpu.make_async_copy(w_hbm, wbuf, w_sem)
    load_w.start()

    barrier = pltpu.get_barrier_semaphore()
    for k in range(1, A):
        pl.semaphore_signal(
            barrier, inc=1, device_id={"patch": over(k) * B + b}, device_id_type=pl.DeviceIdType.MESH
        )
    for k in range(1, B):
        pl.semaphore_signal(
            barrier,
            inc=1,
            device_id={"patch": a * B + lax.rem(b + k, B)},
            device_id_type=pl.DeviceIdType.MESH,
        )
    pl.semaphore_wait(barrier, A + B - 2)

    def cols(group):
        return pl.ds(pl.multiple_of(group * GW, GW), GW)

    def slot(bb, aa):
        return bb * A + aa

    mine = slot(b, a)
    for k in range(1, A):
        go(
            remote(
                stale.at[:, :, cols(over(k))],
                kvbuf.at[mine],
                a2a_send.at[k],
                kv_recv.at[mine],
                over(k),
                b,
            )
        )

    def spread(k):
        s = slot(b, over(k))
        for j in range(1, chips):
            go(
                remote(
                    kvbuf.at[s],
                    kvbuf.at[s],
                    row_send.at[k * chips + j],
                    kv_recv.at[s],
                    a,
                    row_peer(j),
                )
            )
        go(remote(kvbuf.at[s], kvbuf.at[s], sib_send.at[k], kv_recv.at[s], a, sib))

    def forward(k):
        for j in range(1, chips):
            s = slot(row_peer(j), over(k))
            got(kvbuf.at[s], kv_recv.at[s])
            go(remote(kvbuf.at[s], kvbuf.at[s], sib_send.at[j * A + k], kv_recv.at[s], a, sib))

    kvbuf[mine] = stale[:, :, cols(a)]
    spread(0)

    for h in range(HEADS):
        c = slice(h * HD, (h + 1) * HD)
        qsend[:, c] = normed(img_qkv[:, c], img_gain[0:1, :])
    for k in range(1, A):
        go(
            remote(
                qsend.at[:, cols(over(k))], qrecv.at[a], q_send.at[k], q_recv.at[a], over(k), b
            )
        )
    qrecv[a] = qsend[:, cols(a)]

    pad = jnp.zeros((LOC - rows - trows, HD), F32)
    for h in range(HEADS):
        c = slice(h * HD, (h + 1) * HD)
        ck = slice(HW + h * HD, HW + (h + 1) * HD)
        cv = slice(2 * HW + h * HD, 2 * HW + (h + 1) * HD)
        own = normed(img_qkv[:, ck], img_gain[1:2, :])
        fresh[0, :, c] = own
        value = img_qkv[:, cv]
        fresh[1, :, c] = value
        text = normed(txt_qkv[:, ck], txt_gain[1:2, :])
        kloc[:, c] = jnp.concatenate([own.astype(F32), text.astype(F32), pad]).astype(BF16)
        vloc[:, c] = jnp.concatenate(
            [value.astype(F32), txt_qkv[:, cv].astype(F32), pad]
        ).astype(BF16)

    lane = lax.broadcasted_iota(jnp.int32, (1, LOC), 1)
    real = txt_mask[...] == 1
    in_text = (lane >= rows) & (lane < rows + trows) & real
    bias_img = jnp.where((lane < rows) | in_text, 0.0, LOW)
    bias_txt = jnp.where((lane < rows) | (in_text & (me == 0)), 0.0, LOW)

    for g in range(GROUPS):
        logs = []
        for j in range(PER):
            h = g * PER + j
            c = slice(h * HD, (h + 1) * HD)
            query = normed(txt_qkv[:, c], txt_gain[0:1, :])
            mixed, log = soft(nt(query, kloc[:, c]) + bias_txt, vloc[:, c])
            tsend[g, :, j * HD : (j + 1) * HD] = mixed.astype(BF16)
            logs.append(log)
        tsend[g, :, GW:] = pack(logs, trows)
    for k in range(1, A):
        go(remote(tsend.at[over(k)], tz.at[a], tz_send.at[k], tz_recv.at[a], over(k), b))
    tz[a] = tsend[a]

    def local_heads(first, last):
        stats = lloc[...] if first else jnp.zeros((rows, HD), F32)
        spot = lanes_of(rows)
        for h in range(first, last):
            c = slice(h * HD, (h + 1) * HD)
            mixed, log = soft(nt(qsend[:, c], kloc[:, c]) + bias_img, vloc[:, c])
            oloc[:, c] = mixed
            stats = jnp.where(spot == h, log, stats)
        lloc[...] = stats

    def assemble(bb):
        for i in range(A // 2):
            s = slot(bb, 2 * i)
            at = pl.ds(pl.multiple_of(s * rows, 2 * rows), 2 * rows)
            for which, full in ((0, kfull), (1, vfull)):
                full[at, :] = jnp.concatenate(
                    [kvbuf[s, which].astype(F32), kvbuf[s + 1, which].astype(F32)]
                ).astype(BF16)

    step = HEADS // (A - 1)
    for k in range(1, A):
        s = slot(b, over(k))
        got(kvbuf.at[s], kv_recv.at[s])
        spread(k)
        forward(k - 1)
        local_heads((k - 1) * step, k * step)

    def merge_text(blocks, where):
        logs = []
        for j in range(PER):
            c = slice(j * HD, (j + 1) * HD)
            mixed, log = merge(
                [(blk[:, c].astype(F32), unpack(blk, j, trows)) for blk in blocks]
            )
            where(c, mixed.astype(BF16))
            logs.append(log)
        return logs

    for k in range(1, A):
        got(tz.at[over(k)], tz_recv.at[over(k)])

    def put_plane(c, mixed):
        tpl[b, :, c] = mixed

    tpl[b, :, GW:] = pack(merge_text([tz[i] for i in range(A)], put_plane), trows)
    for k in range(1, B):
        go(remote(tpl.at[b], tpl.at[b], tp_send.at[k], tp_recv.at[b], a, lax.rem(b + k, B)))

    assemble(b)
    forward(A - 1)
    for j in range(1, chips):
        assemble(row_peer(j))

    for k in range(1, B):
        other = lax.rem(b + k, B)
        got(tpl.at[other], tp_recv.at[other])

    def put_final(c, mixed):
        tfin[a, :, c] = mixed

    merge_text([tpl[i] for i in range(B)], put_final)
    for k in range(1, A):
        go(remote(tfin.at[a], tfin.at[a], tf_send.at[k], tf_recv.at[a], over(k), b))

    for j in range(chips):
        bb = 2 * lax.rem(chip + j, chips) + 1 - core
        for k in range(A):
            s = slot(bb, over(k))
            got(kvbuf.at[s], kv_recv.at[s])
        assemble(bb)
    for k in range(1, A):
        got(qrecv.at[over(k)], q_recv.at[over(k)])

    place = lax.broadcasted_iota(jnp.int32, (1, n * rows), 1)

    def attend(group, out):
        start = slot(b, group) * rows
        bias = jnp.where((place >= start) & (place < start + rows), LOW, 0.0)
        logs = []
        for j in range(PER):
            c = slice(j * HD, (j + 1) * HD)
            mixed, log = soft(nt(qrecv[group, :, c], kfull[:, c]) + bias, vfull[:, c])
            out[:, c] = mixed.astype(BF16)
            logs.append(log)
        out[:, GW:] = pack(logs, rows)

    for k in range(1, A):
        attend(over(k), osend.at[k])
        go(remote(osend.at[k], orecv.at[a], o_send.at[k], o_recv.at[a], over(k), b))
    attend(a, orecv.at[a])

    for k in range(1, A):
        got(tfin.at[over(k)], tf_recv.at[over(k)])
    text = jnp.concatenate([tfin[i] for i in range(A)], axis=1)
    txt_out[...] = (
        txt_hidden[...].astype(F32)
        + txt_gate[...] * jnp.dot(text, txt_w[...], preferred_element_type=F32)
    ).astype(BF16)

    load_w.wait()
    width = img_hidden.shape[1]
    tile = width // 4
    spot = lanes_of(rows)
    for k in range(A):
        group = over(A - k) if k else a
        if k:
            got(orecv.at[group], o_recv.at[group])
        block = orecv[group]
        base = oloc[:, cols(group)]
        attn = []
        for j in range(PER):
            c = slice(j * HD, (j + 1) * HD)
            log = jnp.sum(
                jnp.where(spot == group * PER + j, lloc[...], 0.0), axis=-1, keepdims=True
            )
            mixed, _ = merge(
                [(block[:, c].astype(F32), unpack(block, j, rows)), (base[:, c], log)]
            )
            attn.append(mixed.astype(BF16))
        attn = jnp.concatenate(attn, axis=1)
        for t in range(4):
            c = slice(t * tile, (t + 1) * tile)
            part = jnp.dot(attn, wbuf[cols(group), c], preferred_element_type=F32)
            if k:
                part = acc[:, c] + part
            if k < A - 1:
                acc[:, c] = part
            else:
                img_out[:, c] = (
                    img_hidden[:, c].astype(F32) + img_gate[:, c] * part
                ).astype(BF16)

    for copy in started:
        copy.wait_send()


def body(
    img_hidden,
    img_qkv,
    stale_kv,
    txt_hidden,
    txt_qkv,
    txt_mask,
    img_qk_gain,
    txt_qk_gain,
    img_gate,
    txt_gate,
    img_out_w,
    txt_out_w,
):
    n = lax.axis_size("patch")
    A = GROUPS
    B = n // A
    rows, width = img_hidden.shape
    trows = txt_qkv.shape[0]
    mask = jnp.pad(txt_mask, (rows, LOC - rows - trows)).reshape(1, LOC)
    vmem = pl.BlockSpec(memory_space=pltpu.VMEM)
    dma = pltpu.SemaphoreType.DMA
    return pl.pallas_call(
        functools.partial(kernel, n),
        out_shape=(
            jax.ShapeDtypeStruct(img_hidden.shape, BF16),
            jax.ShapeDtypeStruct(txt_hidden.shape, BF16),
            jax.ShapeDtypeStruct(stale_kv.shape, BF16),
        ),
        in_specs=[vmem] * 10 + [pl.BlockSpec(memory_space=pl.ANY), vmem],
        out_specs=(vmem, vmem, vmem),
        scratch_shapes=[
            pltpu.VMEM((n, 2, rows, GW), BF16),
            pltpu.VMEM((rows, HW), BF16),
            pltpu.VMEM((A, rows, GW), BF16),
            pltpu.VMEM((n * rows, GW), BF16),
            pltpu.VMEM((n * rows, GW), BF16),
            pltpu.VMEM((LOC, HW), BF16),
            pltpu.VMEM((LOC, HW), BF16),
            pltpu.VMEM((rows, HW), F32),
            pltpu.VMEM((rows, HD), F32),
            pltpu.VMEM((A, rows, GW + HD), BF16),
            pltpu.VMEM((A, rows, GW + HD), BF16),
            pltpu.VMEM((A, trows, GW + HD), BF16),
            pltpu.VMEM((A, trows, GW + HD), BF16),
            pltpu.VMEM((B, trows, GW + HD), BF16),
            pltpu.VMEM((A, trows, GW), BF16),
            pltpu.VMEM(img_out_w.shape, BF16),
            pltpu.VMEM((rows, width), F32),
            dma,
            dma((n,)),
            dma((A,)),
            dma((n,)),
            dma((n,)),
            dma((A,)),
            dma((A,)),
            dma((A,)),
            dma((A,)),
            dma((A,)),
            dma((A,)),
            dma((B,)),
            dma((B,)),
            dma((A,)),
            dma((A,)),
        ],
        compiler_params=pltpu.CompilerParams(
            collective_id=0, has_side_effects=True, vmem_limit_bytes=48 * 1024 * 1024
        ),
        name="joint_attention",
    )(
        img_hidden,
        img_qkv,
        stale_kv,
        txt_hidden,
        txt_qkv,
        mask,
        img_qk_gain,
        txt_qk_gain,
        img_gate.reshape(1, -1),
        txt_gate.reshape(1, -1),
        img_out_w,
        txt_out_w,
    )


def solution(mesh):
    placed = (
        P(("group", "patch"), None),
        P(("group", "patch"), None),
        P(None, ("group", "patch"), None),
        P("group", "patch"),
        P("group", None),
        P("group"),
        P(),
        P(),
        P("group"),
        P(("group", "patch")),
        P(),
        P(None, "patch"),
    )
    return jax.shard_map(
        body,
        mesh=mesh,
        in_specs=placed,
        out_specs=(
            P(("group", "patch"), None),
            P("group", "patch"),
            P(None, ("group", "patch"), None),
        ),
        check_vma=False,
    )
```

time: 202 us -> 53.6 us (0.27)
  local copies, waits for them, and re-layouts: 69.1 us -> 11.7 us
  waiting for transfers between devices: 42.6 us -> 0 us
  blocking collectives: 41 us -> 0 us
  Pallas kernels: 0 us -> 40.7 us
  matrix products: 18.9 us -> 0 us
  between operations: 14.5 us -> 0.66 us
  other arithmetic: 13.3 us -> 0 us
    all_gather x2 -> x0, waiting for transfers between devices: 42.5 us -> none  [the longest x1 42.5 us: body(): piece = lax.all_gather(stale_kv, 'patch', axis=1, tiled=True)]
    all_gather x2 -> x0, blocking collectives: 41 us -> none  [merged(): lax.all_gather(part.astype(kind), axis)]
    pallas_call x0 -> x1, Pallas kernels: none -> 40.7 us  [body(): pl.pallas_call(functools.partial(kernel, n), out_shape=(jax.ShapeDtypeStr...]
    unnamed x27 -> x22, local copies, waits for them, and re-layouts: 34 us -> 11 us
    dot_general x12 -> x0, matrix products: 18.9 us -> none  [the longest x1 6.24 us: body(): jnp.dot(img_attn, img_out_w, preferred_element_type=jnp.float32)]
    slice x1 -> x0, local copies, waits for them, and re-layouts: 15.1 us -> none  [body(): state = absorb(local, query_three, piece[0], piece[1], valid)]
    dynamic_slice x15 -> x0, local copies, waits for them, and re-layouts: 13.7 us -> none  [take(): part[k].astype(own.dtype)]
    add x32 -> x0, other arithmetic: 4.53 us -> none  [the longest x15 4.2 us: join(): first[2] * left[..., None] + second[2] * right[..., None]]
  transfers between devices with their start and end apart: 2 -> 0, of which waited for: 1 -> 0; matrix products, arithmetic and copies ran while one was open for 13% -> 0% of each run, Pallas kernels for 0% -> 0%
where the time goes in v1:
time: 53.6 us; the launch traced here: 53.1 us
  Pallas kernels  40.7 us (76%)
  local copies, waits for them, and re-layouts  11.7 us (22%)
  between operations  0.66 us (1%)
    pallas_call x1, Pallas kernels, body(): pl.pallas_call(functools.partial(kernel, n), out_shape=(jax.ShapeDtypeStr...  40.7 us
    unnamed x22, local copies, waits for them, and re-layouts  11 us

profile of v1, /device:TPU:0, one launch (start us, length us, event | category | flops | bytes accessed | tf_op | source)
XLA Modules:
  0.0 53.1 jit_solution(3187786350690841079)
XLA Ops:
  0.6 0.7 %pad_bitcast_fusion.txt_mask = s32[1,128]{1,0:T(1,128)S(1)} fusion(s32[32]{0:T(128)} %param.17), kind=kLoop, calls=%fused_computation | loop fusion | bytes 640 | tf_op jit(solution)/shard_map/reshape | solution.py:422
  1.4 1.3 %copy.15.txt_w = bf16[1536,192]{1,0:T(8,128)(2,1)S(1)} copy(bf16[1536,192]{0,1:T(8,128)(2,1)} %param.23) | data formatting | bytes 1179648 | tf_op args[11]
  2.7 0.0 copy-start
  2.7 1.1 %copy-done = bf16[72,4608]{1,0:T(8,128)(2,1)S(1)} copy-done((bf16[72,4608]{1,0:T(8,128)(2,1)S(1)}, bf16[72,4608]{1,0:T(8,128)(2,1)}, u32[]{:S(2)}) %copy-start) | copy-done | bytes 663576
  3.8 0.0 copy-start.1
  3.8 1.0 %copy-done.1 = bf16[72,3072]{1,0:T(8,128)(2,1)S(1)} copy-done((bf16[72,3072]{1,0:T(8,128)(2,1)S(1)}, bf16[72,3072]{1,0:T(8,128)(2,1)}, u32[]{:S(2)}) %copy-start.1) | copy-done | bytes 442392
  4.8 0.0 copy-start.2
  4.8 1.0 %copy-done.2 = bf16[2,72,1536]{2,1,0:T(8,128)(2,1)S(1)} copy-done((bf16[2,72,1536]{2,1,0:T(8,128)(2,1)S(1)}, bf16[2,72,1536]{2,1,0:T(8,128)(2,1)}, u32[]{:S(2)}) %copy-start.2) | copy-done | bytes 442392
  5.8 0.0 copy-start.3
  5.8 1.0 %copy-done.3 = bf16[32,4608]{1,0:T(8,128)(2,1)S(1)} copy-done((bf16[32,4608]{1,0:T(8,128)(2,1)S(1)}, bf16[32,4608]{1,0:T(8,128)(2,1)}, u32[]{:S(2)}) %copy-start.3) | copy-done | bytes 294936
  6.8 0.0 copy-start.4
  6.8 0.7 %copy-done.4 = bf16[32,192]{1,0:T(8,128)(2,1)S(1)} copy-done((bf16[32,192]{1,0:T(8,128)(2,1)S(1)}, bf16[32,192]{1,0:T(8,128)(2,1)}, u32[]{:S(2)}) %copy-start.4) | copy-done | bytes 12312
  7.5 0.0 copy-start.5
  7.5 0.7 %copy-done.5 = f32[3072]{0:T(1024)S(1)} copy-done((f32[3072]{0:T(1024)S(1)}, f32[3072]{0:T(1024)}, u32[]{:S(2)}) %copy-start.5) | copy-done | bytes 12312
  8.2 0.0 copy-start.6
  8.2 0.7 %copy-done.6 = f32[2,128]{1,0:T(2,128)S(1)} copy-done((f32[2,128]{1,0:T(2,128)S(1)}, f32[2,128]{1,0:T(2,128)}, u32[]{:S(2)}) %copy-start.6) | copy-done | bytes 1048
  8.9 0.0 copy-start.7
  8.9 0.7 %copy-done.7 = f32[2,128]{1,0:T(2,128)S(1)} copy-done((f32[2,128]{1,0:T(2,128)S(1)}, f32[2,128]{1,0:T(2,128)}, u32[]{:S(2)}) %copy-start.7) | copy-done | bytes 1048
  9.6 0.0 copy-start.8
  9.6 0.7 %copy-done.8 = f32[192]{0:T(256)S(1)} copy-done((f32[192]{0:T(256)S(1)}, f32[192]{0:T(256)}, u32[]{:S(2)}) %copy-start.8) | copy-done | bytes 792
  10.2 40.7 %joint_attention.1 = (bf16[72,3072]{1,0:T(8,128)(2,1)S(1)}, bf16[32,192]{1,0:T(8,128)(2,1)S(1)}, bf16[2,72,1536]{2,1,0:T(8,128)(2,1)S(1)}) custom-call(bf16[72,3072]{1,0:T(8,128)(2,1)S(1)} %copy-done.1, bf16[72,4608]{1,0:T(8,128)(2,1)S(1)} %copy-done, bf16[2,72,1536]{2,1,0:T(8,128)(2,1)S(1)} %copy-done.2, bf16[32,192]{1,0:T(8,128)(2,1)S(1)} %copy-done.4, ...), custom_call_target="tpu_custom_call" | custom-call | tf_op jit(solution)/shard_map/joint_attention/pallas_call | solution.py:425
  51.0 0.8 %copy.19 = bf16[72,3072]{1,0:T(8,128)(2,1)} copy(bf16[72,3072]{1,0:T(8,128)(2,1)S(1)} %get-tuple-element.6) | data formatting | bytes 884736
  51.7 0.6 %copy.20 = bf16[32,192]{1,0:T(8,128)(2,1)} copy(bf16[32,192]{1,0:T(8,128)(2,1)S(1)} %get-tuple-element.7) | data formatting | bytes 24576
  52.4 0.8 %copy.21 = bf16[2,72,1536]{2,1,0:T(8,128)(2,1)} copy(bf16[2,72,1536]{2,1,0:T(8,128)(2,1)S(1)} %get-tuple-element.8) | data formatting | bytes 884736
Async XLA Ops:
  2.7 1.1 %copy-start = (bf16[72,4608]{1,0:T(8,128)(2,1)S(1)}, bf16[72,4608]{1,0:T(8,128)(2,1)}, u32[]{:S(2)}) copy-start(bf16[72,4608]{1,0:T(8,128)(2,1)} %img_qkv.1) | copy-start | bytes 1990660
  3.8 1.0 %copy-start.1 = (bf16[72,3072]{1,0:T(8,128)(2,1)S(1)}, bf16[72,3072]{1,0:T(8,128)(2,1)}, u32[]{:S(2)}) copy-start(bf16[72,3072]{1,0:T(8,128)(2,1)} %img_hidden.1) | copy-start | bytes 1327108
  4.8 1.0 %copy-start.2 = (bf16[2,72,1536]{2,1,0:T(8,128)(2,1)S(1)}, bf16[2,72,1536]{2,1,0:T(8,128)(2,1)}, u32[]{:S(2)}) copy-start(bf16[2,72,1536]{2,1,0:T(8,128)(2,1)} %stale.1) | copy-start | bytes 1327108
  5.8 1.0 %copy-start.3 = (bf16[32,4608]{1,0:T(8,128)(2,1)S(1)}, bf16[32,4608]{1,0:T(8,128)(2,1)}, u32[]{:S(2)}) copy-start(bf16[32,4608]{1,0:T(8,128)(2,1)} %txt_qkv.1) | copy-start | bytes 884740
  6.8 0.7 %copy-start.4 = (bf16[32,192]{1,0:T(8,128)(2,1)S(1)}, bf16[32,192]{1,0:T(8,128)(2,1)}, u32[]{:S(2)}) copy-start(bf16[32,192]{1,0:T(8,128)(2,1)} %txt_hidden.1) | copy-start | bytes 36868
  7.5 0.7 %copy-start.5 = (f32[3072]{0:T(1024)S(1)}, f32[3072]{0:T(1024)}, u32[]{:S(2)}) copy-start(f32[3072]{0:T(1024)} %param.20) | copy-start | bytes 36868
  8.2 0.7 %copy-start.6 = (f32[2,128]{1,0:T(2,128)S(1)}, f32[2,128]{1,0:T(2,128)}, u32[]{:S(2)}) copy-start(f32[2,128]{1,0:T(2,128)} %img_gain.1) | copy-start | bytes 3076
  8.9 0.7 %copy-start.7 = (f32[2,128]{1,0:T(2,128)S(1)}, f32[2,128]{1,0:T(2,128)}, u32[]{:S(2)}) copy-start(f32[2,128]{1,0:T(2,128)} %txt_gain.1) | copy-start | bytes 3076
  9.6 0.7 %copy-start.8 = (f32[192]{0:T(256)S(1)}, f32[192]{0:T(256)}, u32[]{:S(2)}) copy-start(f32[192]{0:T(256)} %param.21) | copy-start | bytes 2308

commit v2 on v1

--- a/solution.py
+++ b/solution.py
@@ -73,9 +73,23 @@
 
 def kernel(
     n,
+    img_hidden_hbm,
+    img_qkv_hbm,
+    stale,
+    txt_hidden_hbm,
+    txt_qkv_hbm,
+    txt_mask_hbm,
+    img_gain_hbm,
+    txt_gain_hbm,
+    img_gate_hbm,
+    txt_gate_hbm,
+    w_hbm,
+    txt_w_hbm,
+    img_out,
+    txt_out,
+    fresh_hbm,
     img_hidden,
     img_qkv,
-    stale,
     txt_hidden,
     txt_qkv,
     txt_mask,
@@ -83,10 +97,8 @@
     txt_gain,
     img_gate,
     txt_gate,
-    w_hbm,
     txt_w,
-    img_out,
-    txt_out,
+    wide_mask,
     fresh,
     kvbuf,
     qsend,
@@ -105,7 +117,9 @@
     tfin,
     wbuf,
     acc,
-    w_sem,
+    load_sem,
+    fresh_sem,
+    own_sem,
     kv_recv,
     a2a_send,
     sib_send,
@@ -158,8 +172,26 @@
         copy.start()
         started.append(copy)
 
-    load_w = pltpu.make_async_copy(w_hbm, wbuf, w_sem)
-    load_w.start()
+    loads = [
+        pltpu.make_async_copy(src, dst, load_sem.at[i])
+        for i, (src, dst) in enumerate(
+            (
+                (img_qkv_hbm, img_qkv),
+                (img_gain_hbm, img_gain),
+                (txt_qkv_hbm, txt_qkv),
+                (txt_gain_hbm, txt_gain),
+                (txt_mask_hbm, txt_mask),
+                (txt_w_hbm, txt_w),
+                (txt_hidden_hbm, txt_hidden),
+                (txt_gate_hbm, txt_gate),
+                (img_hidden_hbm, img_hidden),
+                (img_gate_hbm, img_gate),
+                (w_hbm, wbuf),
+            )
+        )
+    ]
+    for load in loads[:5]:
+        load.start()
 
     barrier = pltpu.get_barrier_semaphore()
     for k in range(1, A):
@@ -173,8 +205,6 @@
             device_id={"patch": a * B + lax.rem(b + k, B)},
             device_id_type=pl.DeviceIdType.MESH,
         )
-    pl.semaphore_wait(barrier, A + B - 2)
-
     def cols(group):
         return pl.ds(pl.multiple_of(group * GW, GW), GW)
 
@@ -182,6 +212,9 @@
         return bb * A + aa
 
     mine = slot(b, a)
+    own_copy = pltpu.make_async_copy(stale.at[:, :, cols(a)], kvbuf.at[mine], own_sem)
+    own_copy.start()
+    pl.semaphore_wait(barrier, A + B - 2)
     for k in range(1, A):
         go(
             remote(
@@ -215,8 +248,12 @@
             got(kvbuf.at[s], kv_recv.at[s])
             go(remote(kvbuf.at[s], kvbuf.at[s], sib_send.at[j * A + k], kv_recv.at[s], a, sib))
 
-    kvbuf[mine] = stale[:, :, cols(a)]
+    own_copy.wait()
     spread(0)
+    for load in loads[5:]:
+        load.start()
+    for load in loads[:2]:
+        load.wait()
 
     for h in range(HEADS):
         c = slice(h * HD, (h + 1) * HD)
@@ -229,6 +266,8 @@
         )
     qrecv[a] = qsend[:, cols(a)]
 
+    for load in loads[2:5]:
+        load.wait()
     pad = jnp.zeros((LOC - rows - trows, HD), F32)
     for h in range(HEADS):
         c = slice(h * HD, (h + 1) * HD)
@@ -239,16 +278,21 @@
         value = img_qkv[:, cv]
         fresh[1, :, c] = value
         text = normed(txt_qkv[:, ck], txt_gain[1:2, :])
-        kloc[:, c] = jnp.concatenate([own.astype(F32), text.astype(F32), pad]).astype(BF16)
+        kloc[:, c] = jnp.concatenate([text.astype(F32), own.astype(F32), pad]).astype(BF16)
         vloc[:, c] = jnp.concatenate(
-            [value.astype(F32), txt_qkv[:, cv].astype(F32), pad]
+            [txt_qkv[:, cv].astype(F32), value.astype(F32), pad]
         ).astype(BF16)
 
+    keep_fresh = pltpu.make_async_copy(fresh, fresh_hbm, fresh_sem)
+    keep_fresh.start()
+
     lane = lax.broadcasted_iota(jnp.int32, (1, LOC), 1)
-    real = txt_mask[...] == 1
-    in_text = (lane >= rows) & (lane < rows + trows) & real
-    bias_img = jnp.where((lane < rows) | in_text, 0.0, LOW)
-    bias_txt = jnp.where((lane < rows) | (in_text & (me == 0)), 0.0, LOW)
+    wide_mask[...] = jnp.zeros((1, LOC), jnp.int32)
+    wide_mask[:, :trows] = txt_mask[...]
+    in_text = wide_mask[...] == 1
+    in_img = (lane >= trows) & (lane < trows + rows)
+    bias_img = jnp.where(in_img | in_text, 0.0, LOW)
+    bias_txt = jnp.where(in_img | (in_text & (me == 0)), 0.0, LOW)
 
     for g in range(GROUPS):
         logs = []
@@ -357,13 +401,14 @@
 
     for k in range(1, A):
         got(tfin.at[over(k)], tf_recv.at[over(k)])
+    for load in loads[5:]:
+        load.wait()
     text = jnp.concatenate([tfin[i] for i in range(A)], axis=1)
     txt_out[...] = (
         txt_hidden[...].astype(F32)
-        + txt_gate[...] * jnp.dot(text, txt_w[...], preferred_element_type=F32)
+        + txt_gate[...] * nt(text, txt_w[...])
     ).astype(BF16)
 
-    load_w.wait()
     width = img_hidden.shape[1]
     tile = width // 4
     spot = lanes_of(rows)
@@ -396,6 +441,7 @@
                     img_hidden[:, c].astype(F32) + img_gate[:, c] * part
                 ).astype(BF16)
 
+    keep_fresh.wait()
     for copy in started:
         copy.wait_send()
 
@@ -419,7 +465,6 @@
     B = n // A
     rows, width = img_hidden.shape
     trows = txt_qkv.shape[0]
-    mask = jnp.pad(txt_mask, (rows, LOC - rows - trows)).reshape(1, LOC)
     vmem = pl.BlockSpec(memory_space=pltpu.VMEM)
     dma = pltpu.SemaphoreType.DMA
     return pl.pallas_call(
@@ -429,9 +474,21 @@
             jax.ShapeDtypeStruct(txt_hidden.shape, BF16),
             jax.ShapeDtypeStruct(stale_kv.shape, BF16),
         ),
-        in_specs=[vmem] * 10 + [pl.BlockSpec(memory_space=pl.ANY), vmem],
-        out_specs=(vmem, vmem, vmem),
+        in_specs=[pl.BlockSpec(memory_space=pltpu.HBM)] * 12,
+        out_specs=(vmem, vmem, pl.BlockSpec(memory_space=pltpu.HBM)),
         scratch_shapes=[
+            pltpu.VMEM(img_hidden.shape, BF16),
+            pltpu.VMEM(img_qkv.shape, BF16),
+            pltpu.VMEM(txt_hidden.shape, BF16),
+            pltpu.VMEM(txt_qkv.shape, BF16),
+            pltpu.VMEM((1, trows), jnp.int32),
+            pltpu.VMEM(img_qk_gain.shape, F32),
+            pltpu.VMEM(txt_qk_gain.shape, F32),
+            pltpu.VMEM((1, width), F32),
+            pltpu.VMEM((1, txt_gate.shape[0]), F32),
+            pltpu.VMEM(txt_out_w.shape[::-1], BF16),
+            pltpu.VMEM((1, LOC), jnp.int32),
+            pltpu.VMEM(stale_kv.shape, BF16),
             pltpu.VMEM((n, 2, rows, GW), BF16),
             pltpu.VMEM((rows, HW), BF16),
             pltpu.VMEM((A, rows, GW), BF16),
@@ -449,6 +506,8 @@
             pltpu.VMEM((A, trows, GW), BF16),
             pltpu.VMEM(img_out_w.shape, BF16),
             pltpu.VMEM((rows, width), F32),
+            dma((11,)),
+            dma,
             dma,
             dma((n,)),
             dma((A,)),
@@ -466,7 +525,7 @@
             dma((A,)),
         ],
         compiler_params=pltpu.CompilerParams(
-            collective_id=0, has_side_effects=True, vmem_limit_bytes=48 * 1024 * 1024
+            collective_id=0, has_side_effects=True, vmem_limit_bytes=64 * 1024 * 1024
         ),
         name="joint_attention",
     )(
@@ -475,13 +534,13 @@
         stale_kv,
         txt_hidden,
         txt_qkv,
-        mask,
+        txt_mask.reshape(1, -1),
         img_qk_gain,
         txt_qk_gain,
         img_gate.reshape(1, -1),
         txt_gate.reshape(1, -1),
         img_out_w,
-        txt_out_w,
+        txt_out_w.T,
     )
 
 

time: 53.6 us -> 47.6 us (0.89)
  local copies, waits for them, and re-layouts: 11.7 us -> 4.93 us
  Pallas kernels: 40.7 us -> 41.8 us
    unnamed x22 -> x3, local copies, waits for them, and re-layouts: 11 us -> 4.93 us
    pallas_call x1, Pallas kernels: 40.7 us -> 41.8 us  [body(): pl.pallas_call(functools.partial(kernel, n), out_shape=(jax.ShapeDtypeStr...]
    reshape x1 -> x0, local copies, waits for them, and re-layouts: 0.73 us -> none  [body(): mask = jnp.pad(txt_mask, (rows, LOC - rows - trows)).reshape(1, LOC)]
where the time goes in v2:
time: 47.6 us; the launch traced here: 47.3 us
  Pallas kernels  41.8 us (88%)
  local copies, waits for them, and re-layouts  4.93 us (10%)
  between operations  0.64 us (1%)
    pallas_call x1, Pallas kernels, body(): pl.pallas_call(functools.partial(kernel, n), out_shape=(jax.ShapeDtypeStr...  41.8 us
    unnamed x3, local copies, waits for them, and re-layouts  4.93 us

profile of v2, /device:TPU:0, one launch (start us, length us, event | category | flops | bytes accessed | tf_op | source)
XLA Modules:
  0.0 47.3 jit_solution(4069511872899391099)
XLA Ops:
  0.6 41.8 %joint_attention.1 = (bf16[72,3072]{1,0:T(8,128)(2,1)}, bf16[32,192]{1,0:T(8,128)(2,1)}, bf16[2,72,1536]{2,1,0:T(8,128)(2,1)}) custom-call(bf16[72,3072]{1,0:T(8,128)(2,1)} %img_hidden_hbm.1, bf16[72,4608]{1,0:T(8,128)(2,1)} %img_qkv_hbm.1, bf16[2,72,1536]{2,1,0:T(8,128)(2,1)} %stale.1, bf16[32,192]{1,0:T(8,128)(2,1)} %txt_hidden_hbm.1, ...), custom_call_target="tpu_custom_call" | custom-call | tf_op jit(solution)/shard_map/joint_attention/pallas_call | solution.py:470
  42.4 1.8 %copy.18 = bf16[72,3072]{1,0:T(8,128)(2,1)} copy(bf16[72,3072]{1,0:T(8,128)(2,1)} %get-tuple-element.6) | data formatting | bytes 884736
  44.2 1.3 %copy.19 = bf16[32,192]{1,0:T(8,128)(2,1)} copy(bf16[32,192]{1,0:T(8,128)(2,1)} %get-tuple-element.7) | data formatting | bytes 24576
  45.5 1.8 %copy.20 = bf16[2,72,1536]{2,1,0:T(8,128)(2,1)} copy(bf16[2,72,1536]{2,1,0:T(8,128)(2,1)} %get-tuple-element.8) | data formatting | bytes 884736

commit v3 on v2

--- a/solution.py
+++ b/solution.py
@@ -215,42 +215,53 @@
     own_copy = pltpu.make_async_copy(stale.at[:, :, cols(a)], kvbuf.at[mine], own_sem)
     own_copy.start()
     pl.semaphore_wait(barrier, A + B - 2)
-    for k in range(1, A):
-        go(
-            remote(
-                stale.at[:, :, cols(over(k))],
-                kvbuf.at[mine],
-                a2a_send.at[k],
-                kv_recv.at[mine],
-                over(k),
-                b,
+    def exchange(which):
+        for k in range(1, A):
+            go(
+                remote(
+                    stale.at[which, :, cols(over(k))],
+                    kvbuf.at[mine, which],
+                    a2a_send.at[k, which],
+                    kv_recv.at[mine, which],
+                    over(k),
+                    b,
+                )
             )
-        )
-
-    def spread(k):
+        return started[-(A - 1) :]
+
+    def left(copies):
+        for copy in copies:
+            copy.wait_send()
+        started[:] = [copy for copy in started if all(copy is not c for c in copies)]
+
+    def spread(k, which):
         s = slot(b, over(k))
+        part = kvbuf.at[s, which]
         for j in range(1, chips):
             go(
                 remote(
-                    kvbuf.at[s],
-                    kvbuf.at[s],
-                    row_send.at[k * chips + j],
-                    kv_recv.at[s],
+                    part,
+                    part,
+                    row_send.at[k * chips + j, which],
+                    kv_recv.at[s, which],
                     a,
                     row_peer(j),
                 )
             )
-        go(remote(kvbuf.at[s], kvbuf.at[s], sib_send.at[k], kv_recv.at[s], a, sib))
-
-    def forward(k):
+        go(remote(part, part, sib_send.at[k, which], kv_recv.at[s, which], a, sib))
+
+    def forward(k, which):
         for j in range(1, chips):
             s = slot(row_peer(j), over(k))
-            got(kvbuf.at[s], kv_recv.at[s])
-            go(remote(kvbuf.at[s], kvbuf.at[s], sib_send.at[j * A + k], kv_recv.at[s], a, sib))
-
+            part = kvbuf.at[s, which]
+            got(part, kv_recv.at[s, which])
+            go(remote(part, part, sib_send.at[j * A + k, which], kv_recv.at[s, which], a, sib))
+
+    keys_away = exchange(0)
     own_copy.wait()
-    spread(0)
-    for load in loads[5:]:
+    spread(0, 0)
+    spread(0, 1)
+    for load in loads[5:10]:
         load.start()
     for load in loads[:2]:
         load.wait()
@@ -258,13 +269,10 @@
     for h in range(HEADS):
         c = slice(h * HD, (h + 1) * HD)
         qsend[:, c] = normed(img_qkv[:, c], img_gain[0:1, :])
-    for k in range(1, A):
-        go(
-            remote(
-                qsend.at[:, cols(over(k))], qrecv.at[a], q_send.at[k], q_recv.at[a], over(k), b
-            )
-        )
     qrecv[a] = qsend[:, cols(a)]
+
+    left(keys_away)
+    values_away = exchange(1)
 
     for load in loads[2:5]:
         load.wait()
@@ -304,8 +312,6 @@
             tsend[g, :, j * HD : (j + 1) * HD] = mixed.astype(BF16)
             logs.append(log)
         tsend[g, :, GW:] = pack(logs, trows)
-    for k in range(1, A):
-        go(remote(tsend.at[over(k)], tz.at[a], tz_send.at[k], tz_recv.at[a], over(k), b))
     tz[a] = tsend[a]
 
     def local_heads(first, last):
@@ -328,12 +334,33 @@
                 ).astype(BF16)
 
     step = HEADS // (A - 1)
+    forward(0, 0)
+    forward(0, 1)
     for k in range(1, A):
         s = slot(b, over(k))
-        got(kvbuf.at[s], kv_recv.at[s])
-        spread(k)
-        forward(k - 1)
+        got(kvbuf.at[s, 0], kv_recv.at[s, 0])
+        spread(k, 0)
+    left(values_away)
+    for k in range(1, A):
+        go(
+            remote(
+                qsend.at[:, cols(over(k))], qrecv.at[a], q_send.at[k], q_recv.at[a], over(k), b
+            )
+        )
+    queries_away = started[-(A - 1) :]
+    for k in range(1, A):
+        s = slot(b, over(k))
+        got(kvbuf.at[s, 1], kv_recv.at[s, 1])
+        spread(k, 1)
+    left(queries_away)
+    for k in range(1, A):
+        go(remote(tsend.at[over(k)], tz.at[a], tz_send.at[k], tz_recv.at[a], over(k), b))
+    loads[10].start()
+    for k in range(1, A):
+        forward(k, 0)
         local_heads((k - 1) * step, k * step)
+    for k in range(1, A):
+        forward(k, 1)
 
     def merge_text(blocks, where):
         logs = []
@@ -346,6 +373,9 @@
             logs.append(log)
         return logs
 
+    for j in range(chips):
+        assemble(row_peer(j) if j else b)
+
     for k in range(1, A):
         got(tz.at[over(k)], tz_recv.at[over(k)])
 
@@ -355,28 +385,13 @@
     tpl[b, :, GW:] = pack(merge_text([tz[i] for i in range(A)], put_plane), trows)
     for k in range(1, B):
         go(remote(tpl.at[b], tpl.at[b], tp_send.at[k], tp_recv.at[b], a, lax.rem(b + k, B)))
-
-    assemble(b)
-    forward(A - 1)
-    for j in range(1, chips):
-        assemble(row_peer(j))
-
-    for k in range(1, B):
-        other = lax.rem(b + k, B)
-        got(tpl.at[other], tp_recv.at[other])
-
-    def put_final(c, mixed):
-        tfin[a, :, c] = mixed
-
-    merge_text([tpl[i] for i in range(B)], put_final)
-    for k in range(1, A):
-        go(remote(tfin.at[a], tfin.at[a], tf_send.at[k], tf_recv.at[a], over(k), b))
 
     for j in range(chips):
         bb = 2 * lax.rem(chip + j, chips) + 1 - core
         for k in range(A):
             s = slot(bb, over(k))
-            got(kvbuf.at[s], kv_recv.at[s])
+            got(kvbuf.at[s, 0], kv_recv.at[s, 0])
+            got(kvbuf.at[s, 1], kv_recv.at[s, 1])
         assemble(bb)
     for k in range(1, A):
         got(qrecv.at[over(k)], q_recv.at[over(k)])
@@ -394,26 +409,35 @@
             logs.append(log)
         out[:, GW:] = pack(logs, rows)
 
+    def put_final(c, mixed):
+        tfin[a, :, c] = mixed
+
     for k in range(1, A):
         attend(over(k), osend.at[k])
         go(remote(osend.at[k], orecv.at[a], o_send.at[k], o_recv.at[a], over(k), b))
+        if k == 1:
+            for i in range(1, B):
+                other = lax.rem(b + i, B)
+                got(tpl.at[other], tp_recv.at[other])
+            merge_text([tpl[i] for i in range(B)], put_final)
+            for i in range(1, A):
+                go(remote(tfin.at[a], tfin.at[a], tf_send.at[i], tf_recv.at[a], over(i), b))
     attend(a, orecv.at[a])
 
-    for k in range(1, A):
-        got(tfin.at[over(k)], tf_recv.at[over(k)])
     for load in loads[5:]:
         load.wait()
-    text = jnp.concatenate([tfin[i] for i in range(A)], axis=1)
-    txt_out[...] = (
-        txt_hidden[...].astype(F32)
-        + txt_gate[...] * nt(text, txt_w[...])
-    ).astype(BF16)
-
     width = img_hidden.shape[1]
     tile = width // 4
     spot = lanes_of(rows)
     for k in range(A):
         group = over(A - k) if k else a
+        if k == A - 1:
+            for i in range(1, A):
+                got(tfin.at[over(i)], tf_recv.at[over(i)])
+            text = jnp.concatenate([tfin[i] for i in range(A)], axis=1)
+            txt_out[...] = (
+                txt_hidden[...].astype(F32) + txt_gate[...] * nt(text, txt_w[...])
+            ).astype(BF16)
         if k:
             got(orecv.at[group], o_recv.at[group])
         block = orecv[group]
@@ -446,6 +470,24 @@
         copy.wait_send()
 
 
+def keep(count, *refs):
+    sources, results, held = (refs[i * count : (i + 1) * count] for i in range(3))
+    in_sem, out_sem = refs[3 * count :]
+    loads = [
+        pltpu.make_async_copy(sources[i], held[i], in_sem.at[i]) for i in range(count)
+    ]
+    stores = [
+        pltpu.make_async_copy(held[i], results[i], out_sem.at[i]) for i in range(count)
+    ]
+    for load in loads:
+        load.start()
+    for load, store in zip(loads, stores):
+        load.wait()
+        store.start()
+    for store in stores:
+        store.wait()
+
+
 def body(
     img_hidden,
     img_qkv,
@@ -467,7 +509,7 @@
     trows = txt_qkv.shape[0]
     vmem = pl.BlockSpec(memory_space=pltpu.VMEM)
     dma = pltpu.SemaphoreType.DMA
-    return pl.pallas_call(
+    results = pl.pallas_call(
         functools.partial(kernel, n),
         out_shape=(
             jax.ShapeDtypeStruct(img_hidden.shape, BF16),
@@ -509,10 +551,10 @@
             dma((11,)),
             dma,
             dma,
-            dma((n,)),
-            dma((A,)),
-            dma((n,)),
-            dma((n,)),
+            dma((n, 2)),
+            dma((A, 2)),
+            dma((n, 2)),
+            dma((n, 2)),
             dma((A,)),
             dma((A,)),
             dma((A,)),
@@ -542,6 +584,16 @@
         img_out_w,
         txt_out_w.T,
     )
+    hbm = pl.BlockSpec(memory_space=pltpu.HBM)
+    return pl.pallas_call(
+        functools.partial(keep, 3),
+        out_shape=tuple(jax.ShapeDtypeStruct(x.shape, x.dtype) for x in results),
+        in_specs=[hbm] * 3,
+        out_specs=(hbm,) * 3,
+        scratch_shapes=[pltpu.VMEM(x.shape, x.dtype) for x in results] + [dma((3,)), dma((3,))],
+        compiler_params=pltpu.CompilerParams(vmem_limit_bytes=64 * 1024 * 1024),
+        name="keep_results",
+    )(*results)
 
 
 def solution(mesh):

time: 47.6 us -> 42.8 us (0.90)
  local copies, waits for them, and re-layouts: 4.93 us -> 0 us
    unnamed x3 -> x0, local copies, waits for them, and re-layouts: 4.93 us -> none
    pallas_call x0 -> x1, Pallas kernels: none -> 1.98 us  [body(): pl.pallas_call(functools.partial(keep, 3), out_shape=tuple((jax.ShapeDtyp...]
    pallas_call x1, Pallas kernels: 41.8 us -> 40 us  [body(): pl.pallas_call(functools.partial(kernel, n), out_shape=(jax.ShapeDtypeStr...]
where the time goes in v3:
time: 42.8 us; the launch traced here: 42.6 us
  Pallas kernels  42 us (98%)
  between operations  0.64 us (1%)
    pallas_call x1, Pallas kernels, body(): pl.pallas_call(functools.partial(kernel, n), out_shape=(jax.ShapeDtypeStr...  40 us
    pallas_call x1, Pallas kernels, body(): pl.pallas_call(functools.partial(keep, 3), out_shape=tuple((jax.ShapeDtyp...  1.98 us

profile of v3, /device:TPU:0, one launch (start us, length us, event | category | flops | bytes accessed | tf_op | source)
XLA Modules:
  0.0 42.6 jit_solution(9505393615681926226)
XLA Ops:
  0.6 40.0 %joint_attention.1 = (bf16[72,3072]{1,0:T(8,128)(2,1)}, bf16[32,192]{1,0:T(8,128)(2,1)}, bf16[2,72,1536]{2,1,0:T(8,128)(2,1)}) custom-call(bf16[72,3072]{1,0:T(8,128)(2,1)} %img_hidden_hbm.1, bf16[72,4608]{1,0:T(8,128)(2,1)} %img_qkv_hbm.1, bf16[2,72,1536]{2,1,0:T(8,128)(2,1)} %stale.1, bf16[32,192]{1,0:T(8,128)(2,1)} %txt_hidden_hbm.1, ...), custom_call_target="tpu_custom_call" | custom-call | tf_op jit(solution)/shard_map/joint_attention/pallas_call | solution.py:512
  40.7 2.0 %keep_results.1 = (bf16[72,3072]{1,0:T(8,128)(2,1)}, bf16[32,192]{1,0:T(8,128)(2,1)}, bf16[2,72,1536]{2,1,0:T(8,128)(2,1)}) custom-call(bf16[72,3072]{1,0:T(8,128)(2,1)} %get-tuple-element.6.refs_0_, bf16[32,192]{1,0:T(8,128)(2,1)} %get-tuple-element.7.refs_1_, bf16[2,72,1536]{2,1,0:T(8,128)(2,1)} %get-tuple-element.8.refs_2_), custom_call_target="tpu_custom_call" | custom-call | tf_op jit(solution)/shard_map/keep_results/pallas_call | solution.py:588

commit v4 on v3

--- a/solution.py
+++ b/solution.py
@@ -15,6 +15,7 @@
 GW = PER * HD
 HW = HEADS * HD
 LOC = 128
+STAT = 16
 LOW = -1e30
 SCALE = 1.0 / math.sqrt(HD)
 LOG2E = 1.0 / math.log(2.0)
@@ -43,7 +44,7 @@
     return mixed / total, top * SCALE + jnp.log(total)
 
 
-def pack(logs, rows):
+def split(logs, rows):
     lane = lanes_of(rows)
     out = jnp.zeros((rows, HD), F32)
     for j, log in enumerate(logs):
@@ -52,15 +53,32 @@
         mid = rest.astype(BF16).astype(F32)
         for i, part in enumerate((high, mid, rest - mid)):
             out = jnp.where(lane == 3 * j + i, part, out)
-    return out.astype(BF16)
-
-
-def unpack(block, j, rows):
+    return out
+
+
+def pack(logs, rows):
+    return split(logs, rows).astype(BF16)
+
+
+def pack_across(logs, rows):
+    full = jnp.concatenate([split(logs, rows), jnp.zeros((HD - rows, HD), F32)])
+    return full.T[:STAT].astype(BF16)
+
+
+def unpack_across(stats, rows):
+    full = jnp.concatenate([stats.astype(F32), jnp.zeros((HD - STAT, HD), F32)])
+    return full.T[:rows]
+
+
+def joined(stats, j, rows):
     lane = lanes_of(rows)
-    stats = block[:, GW : GW + HD].astype(F32)
     return jnp.sum(
         jnp.where((lane >= 3 * j) & (lane < 3 * j + 3), stats, 0.0), axis=-1, keepdims=True
     )
+
+
+def unpack(block, j, rows):
+    return joined(block[:, GW : GW + HD].astype(F32), j, rows)
 
 
 def merge(parts):
@@ -111,6 +129,8 @@
     lloc,
     osend,
     orecv,
+    ssend,
+    srecv,
     tsend,
     tz,
     tpl,
@@ -128,6 +148,8 @@
     q_recv,
     o_send,
     o_recv,
+    s_send,
+    s_recv,
     tz_send,
     tz_recv,
     tp_send,
@@ -312,55 +334,33 @@
             tsend[g, :, j * HD : (j + 1) * HD] = mixed.astype(BF16)
             logs.append(log)
         tsend[g, :, GW:] = pack(logs, trows)
-    tz[a] = tsend[a]
-
-    def local_heads(first, last):
-        stats = lloc[...] if first else jnp.zeros((rows, HD), F32)
-        spot = lanes_of(rows)
-        for h in range(first, last):
-            c = slice(h * HD, (h + 1) * HD)
-            mixed, log = soft(nt(qsend[:, c], kloc[:, c]) + bias_img, vloc[:, c])
-            oloc[:, c] = mixed
-            stats = jnp.where(spot == h, log, stats)
-        lloc[...] = stats
-
-    def assemble(bb):
-        for i in range(A // 2):
-            s = slot(bb, 2 * i)
-            at = pl.ds(pl.multiple_of(s * rows, 2 * rows), 2 * rows)
-            for which, full in ((0, kfull), (1, vfull)):
-                full[at, :] = jnp.concatenate(
-                    [kvbuf[s, which].astype(F32), kvbuf[s + 1, which].astype(F32)]
-                ).astype(BF16)
-
-    step = HEADS // (A - 1)
-    forward(0, 0)
-    forward(0, 1)
-    for k in range(1, A):
-        s = slot(b, over(k))
-        got(kvbuf.at[s, 0], kv_recv.at[s, 0])
-        spread(k, 0)
-    left(values_away)
-    for k in range(1, A):
-        go(
-            remote(
-                qsend.at[:, cols(over(k))], qrecv.at[a], q_send.at[k], q_recv.at[a], over(k), b
-            )
-        )
-    queries_away = started[-(A - 1) :]
-    for k in range(1, A):
-        s = slot(b, over(k))
-        got(kvbuf.at[s, 1], kv_recv.at[s, 1])
-        spread(k, 1)
-    left(queries_away)
-    for k in range(1, A):
-        go(remote(tsend.at[over(k)], tz.at[a], tz_send.at[k], tz_recv.at[a], over(k), b))
-    loads[10].start()
-    for k in range(1, A):
-        forward(k, 0)
-        local_heads((k - 1) * step, k * step)
-    for k in range(1, A):
-        forward(k, 1)
+
+    def only(condition, act):
+        if B == A:
+            act()
+        else:
+            pl.when(condition)(act)
+
+    def beside(k):
+        return lax.rem(b + k, B)
+
+    def text_part(k):
+        t = beside(k)
+        return remote(tsend.at[t], tpl.at[b], tp_send.at[k], tp_recv.at[b], a, t)
+
+    def text_group(k):
+        return remote(tz.at[a], tz.at[a], tz_send.at[k], tz_recv.at[a], over(k), b)
+
+    def text_final(k):
+        return remote(tfin.at[b], tfin.at[b], tf_send.at[k], tf_recv.at[b], a, beside(k))
+
+    for k in range(1, B):
+        only(beside(k) < A, lambda k=k: text_part(k).start())
+
+    def own_part():
+        tpl[b] = tsend[b]
+
+    only(b < A, own_part)
 
     def merge_text(blocks, where):
         logs = []
@@ -373,18 +373,77 @@
             logs.append(log)
         return logs
 
+    def over_plane():
+        for k in range(1, B):
+            got(tpl.at[beside(k)], tp_recv.at[beside(k)])
+
+        def put(c, mixed):
+            tz[a, :, c] = mixed
+
+        tz[a, :, GW:] = pack(merge_text([tpl[i] for i in range(B)], put), trows)
+        for k in range(1, A):
+            text_group(k).start()
+
+    def over_z():
+        for k in range(1, A):
+            got(tz.at[over(k)], tz_recv.at[over(k)])
+
+        def put(c, mixed):
+            tfin[b, :, c] = mixed
+
+        merge_text([tz[i] for i in range(A)], put)
+        for k in range(1, B):
+            text_final(k).start()
+
+    def local_heads(first, last):
+        stats = lloc[...] if first else jnp.zeros((rows, HD), F32)
+        spot = lanes_of(rows)
+        for h in range(first, last):
+            c = slice(h * HD, (h + 1) * HD)
+            mixed, log = soft(nt(qsend[:, c], kloc[:, c]) + bias_img, vloc[:, c])
+            oloc[:, c] = mixed
+            stats = jnp.where(spot == h, log, stats)
+        lloc[...] = stats
+
+    def assemble(bb):
+        for i in range(A // 2):
+            s = slot(bb, 2 * i)
+            at = pl.ds(pl.multiple_of(s * rows, 2 * rows), 2 * rows)
+            for which, full in ((0, kfull), (1, vfull)):
+                full[at, :] = jnp.concatenate(
+                    [kvbuf[s, which].astype(F32), kvbuf[s + 1, which].astype(F32)]
+                ).astype(BF16)
+
+    step = HEADS // (A - 1)
+    forward(0, 0)
+    forward(0, 1)
+    for k in range(1, A):
+        s = slot(b, over(k))
+        got(kvbuf.at[s, 0], kv_recv.at[s, 0])
+        spread(k, 0)
+    left(values_away)
+    for k in range(1, A):
+        go(
+            remote(
+                qsend.at[:, cols(over(k))], qrecv.at[a], q_send.at[k], q_recv.at[a], over(k), b
+            )
+        )
+    queries_away = started[-(A - 1) :]
+    for k in range(1, A):
+        s = slot(b, over(k))
+        got(kvbuf.at[s, 1], kv_recv.at[s, 1])
+        spread(k, 1)
+    left(queries_away)
+    only(b < A, over_plane)
+    loads[10].start()
+    for k in range(1, A):
+        forward(k, 0)
+        local_heads((k - 1) * step, k * step)
+    for k in range(1, A):
+        forward(k, 1)
+
     for j in range(chips):
         assemble(row_peer(j) if j else b)
-
-    for k in range(1, A):
-        got(tz.at[over(k)], tz_recv.at[over(k)])
-
-    def put_plane(c, mixed):
-        tpl[b, :, c] = mixed
-
-    tpl[b, :, GW:] = pack(merge_text([tz[i] for i in range(A)], put_plane), trows)
-    for k in range(1, B):
-        go(remote(tpl.at[b], tpl.at[b], tp_send.at[k], tp_recv.at[b], a, lax.rem(b + k, B)))
 
     for j in range(chips):
         bb = 2 * lax.rem(chip + j, chips) + 1 - core
@@ -398,7 +457,7 @@
 
     place = lax.broadcasted_iota(jnp.int32, (1, n * rows), 1)
 
-    def attend(group, out):
+    def attend(group, out, stats):
         start = slot(b, group) * rows
         bias = jnp.where((place >= start) & (place < start + rows), LOW, 0.0)
         logs = []
@@ -407,22 +466,15 @@
             mixed, log = soft(nt(qrecv[group, :, c], kfull[:, c]) + bias, vfull[:, c])
             out[:, c] = mixed.astype(BF16)
             logs.append(log)
-        out[:, GW:] = pack(logs, rows)
-
-    def put_final(c, mixed):
-        tfin[a, :, c] = mixed
-
-    for k in range(1, A):
-        attend(over(k), osend.at[k])
+        stats[...] = pack_across(logs, rows)
+
+    for k in range(1, A):
+        attend(over(k), osend.at[k], ssend.at[k])
+        go(remote(ssend.at[k], srecv.at[a], s_send.at[k], s_recv.at[a], over(k), b))
         go(remote(osend.at[k], orecv.at[a], o_send.at[k], o_recv.at[a], over(k), b))
         if k == 1:
-            for i in range(1, B):
-                other = lax.rem(b + i, B)
-                got(tpl.at[other], tp_recv.at[other])
-            merge_text([tpl[i] for i in range(B)], put_final)
-            for i in range(1, A):
-                go(remote(tfin.at[a], tfin.at[a], tf_send.at[i], tf_recv.at[a], over(i), b))
-    attend(a, orecv.at[a])
+            only(b < A, over_z)
+    attend(a, orecv.at[a], srecv.at[a])
 
     for load in loads[5:]:
         load.wait()
@@ -432,15 +484,18 @@
     for k in range(A):
         group = over(A - k) if k else a
         if k == A - 1:
-            for i in range(1, A):
-                got(tfin.at[over(i)], tf_recv.at[over(i)])
+            for i in range(1, B):
+                t = beside(i)
+                only(t < A, lambda t=t: got(tfin.at[t], tf_recv.at[t]))
             text = jnp.concatenate([tfin[i] for i in range(A)], axis=1)
             txt_out[...] = (
                 txt_hidden[...].astype(F32) + txt_gate[...] * nt(text, txt_w[...])
             ).astype(BF16)
         if k:
             got(orecv.at[group], o_recv.at[group])
+            got(srecv.at[group], s_recv.at[group])
         block = orecv[group]
+        stats = unpack_across(srecv[group], rows)
         base = oloc[:, cols(group)]
         attn = []
         for j in range(PER):
@@ -449,7 +504,7 @@
                 jnp.where(spot == group * PER + j, lloc[...], 0.0), axis=-1, keepdims=True
             )
             mixed, _ = merge(
-                [(block[:, c].astype(F32), unpack(block, j, rows)), (base[:, c], log)]
+                [(block[:, c].astype(F32), joined(stats, j, rows)), (base[:, c], log)]
             )
             attn.append(mixed.astype(BF16))
         attn = jnp.concatenate(attn, axis=1)
@@ -465,6 +520,15 @@
                     img_hidden[:, c].astype(F32) + img_gate[:, c] * part
                 ).astype(BF16)
 
+    def text_left():
+        for k in range(1, A):
+            text_group(k).wait_send()
+        for k in range(1, B):
+            text_final(k).wait_send()
+
+    for k in range(1, B):
+        only(beside(k) < A, lambda k=k: text_part(k).wait_send())
+    only(b < A, text_left)
     keep_fresh.wait()
     for copy in started:
         copy.wait_send()
@@ -540,8 +604,10 @@
             pltpu.VMEM((LOC, HW), BF16),
             pltpu.VMEM((rows, HW), F32),
             pltpu.VMEM((rows, HD), F32),
-            pltpu.VMEM((A, rows, GW + HD), BF16),
-            pltpu.VMEM((A, rows, GW + HD), BF16),
+            pltpu.VMEM((A, rows, GW), BF16),
+            pltpu.VMEM((A, rows, GW), BF16),
+            pltpu.VMEM((A, STAT, HD), BF16),
+            pltpu.VMEM((A, STAT, HD), BF16),
             pltpu.VMEM((A, trows, GW + HD), BF16),
             pltpu.VMEM((A, trows, GW + HD), BF16),
             pltpu.VMEM((B, trows, GW + HD), BF16),
@@ -561,9 +627,11 @@
             dma((A,)),
             dma((A,)),
             dma((A,)),
+            dma((A,)),
+            dma((A,)),
             dma((B,)),
             dma((B,)),
-            dma((A,)),
+            dma((B,)),
             dma((A,)),
         ],
         compiler_params=pltpu.CompilerParams(

time: 42.8 us -> 39.3 us (0.918)
  Pallas kernels: 42 us -> 38.5 us
    pallas_call x1, Pallas kernels: 40 us -> 36.5 us  [body(): pl.pallas_call(functools.partial(kernel, n), out_shape=(jax.ShapeDtypeStr...]
where the time goes in v4:
time: 39.3 us; the launch traced here: 39.1 us
  Pallas kernels  38.5 us (98%)
  between operations  0.64 us (2%)
    pallas_call x1, Pallas kernels, body(): pl.pallas_call(functools.partial(kernel, n), out_shape=(jax.ShapeDtypeStr...  36.5 us
    pallas_call x1, Pallas kernels, body(): pl.pallas_call(functools.partial(keep, 3), out_shape=tuple((jax.ShapeDtyp...  1.98 us

profile of v4, /device:TPU:0, one launch (start us, length us, event | category | flops | bytes accessed | tf_op | source)
XLA Modules:
  0.0 39.1 jit_solution(10005584454955059620)
XLA Ops:
  0.6 36.5 %joint_attention.1 = (bf16[72,3072]{1,0:T(8,128)(2,1)}, bf16[32,192]{1,0:T(8,128)(2,1)}, bf16[2,72,1536]{2,1,0:T(8,128)(2,1)}) custom-call(bf16[72,3072]{1,0:T(8,128)(2,1)} %img_hidden_hbm.1, bf16[72,4608]{1,0:T(8,128)(2,1)} %img_qkv_hbm.1, bf16[2,72,1536]{2,1,0:T(8,128)(2,1)} %stale.1, bf16[32,192]{1,0:T(8,128)(2,1)} %txt_hidden_hbm.1, ...), custom_call_target="tpu_custom_call" | custom-call | tf_op jit(solution)/shard_map/joint_attention/pallas_call | solution.py:576
  37.2 2.0 %keep_results.1 = (bf16[72,3072]{1,0:T(8,128)(2,1)}, bf16[32,192]{1,0:T(8,128)(2,1)}, bf16[2,72,1536]{2,1,0:T(8,128)(2,1)}) custom-call(bf16[72,3072]{1,0:T(8,128)(2,1)} %get-tuple-element.6.refs_0_, bf16[32,192]{1,0:T(8,128)(2,1)} %get-tuple-element.7.refs_1_, bf16[2,72,1536]{2,1,0:T(8,128)(2,1)} %get-tuple-element.8.refs_2_), custom_call_target="tpu_custom_call" | custom-call | tf_op jit(solution)/shard_map/keep_results/pallas_call | solution.py:656

commit v5 on v4

--- a/solution.py
+++ b/solution.py
@@ -316,6 +316,13 @@
     keep_fresh = pltpu.make_async_copy(fresh, fresh_hbm, fresh_sem)
     keep_fresh.start()
 
+    forward(0, 0)
+    forward(0, 1)
+    for k in range(1, A):
+        s = slot(b, over(k))
+        got(kvbuf.at[s, 0], kv_recv.at[s, 0])
+        spread(k, 0)
+
     lane = lax.broadcasted_iota(jnp.int32, (1, LOC), 1)
     wide_mask[...] = jnp.zeros((1, LOC), jnp.int32)
     wide_mask[:, :trows] = txt_mask[...]
@@ -415,12 +422,6 @@
                 ).astype(BF16)
 
     step = HEADS // (A - 1)
-    forward(0, 0)
-    forward(0, 1)
-    for k in range(1, A):
-        s = slot(b, over(k))
-        got(kvbuf.at[s, 0], kv_recv.at[s, 0])
-        spread(k, 0)
     left(values_away)
     for k in range(1, A):
         go(

time: 39.3 us -> 38.7 us (0.985)
  Pallas kernels: 38.5 us -> 37.9 us
    pallas_call x1, Pallas kernels: 36.5 us -> 35.9 us  [body(): pl.pallas_call(functools.partial(kernel, n), out_shape=(jax.ShapeDtypeStr...]
where the time goes in v5:
time: 38.7 us; the launch traced here: 38.5 us
  Pallas kernels  37.9 us (98%)
  between operations  0.64 us (2%)
    pallas_call x1, Pallas kernels, body(): pl.pallas_call(functools.partial(kernel, n), out_shape=(jax.ShapeDtypeStr...  35.9 us
    pallas_call x1, Pallas kernels, body(): pl.pallas_call(functools.partial(keep, 3), out_shape=tuple((jax.ShapeDtyp...  1.98 us

profile of v5, /device:TPU:0, one launch (start us, length us, event | category | flops | bytes accessed | tf_op | source)
XLA Modules:
  0.0 38.5 jit_solution(4967008807316723938)
XLA Ops:
  0.6 35.9 %joint_attention.1 = (bf16[72,3072]{1,0:T(8,128)(2,1)}, bf16[32,192]{1,0:T(8,128)(2,1)}, bf16[2,72,1536]{2,1,0:T(8,128)(2,1)}) custom-call(bf16[72,3072]{1,0:T(8,128)(2,1)} %img_hidden_hbm.1, bf16[72,4608]{1,0:T(8,128)(2,1)} %img_qkv_hbm.1, bf16[2,72,1536]{2,1,0:T(8,128)(2,1)} %stale.1, bf16[32,192]{1,0:T(8,128)(2,1)} %txt_hidden_hbm.1, ...), custom_call_target="tpu_custom_call" | custom-call | tf_op jit(solution)/shard_map/joint_attention/pallas_call | solution.py:577
  36.5 2.0 %keep_results.1 = (bf16[72,3072]{1,0:T(8,128)(2,1)}, bf16[32,192]{1,0:T(8,128)(2,1)}, bf16[2,72,1536]{2,1,0:T(8,128)(2,1)}) custom-call(bf16[72,3072]{1,0:T(8,128)(2,1)} %get-tuple-element.6.refs_0_, bf16[32,192]{1,0:T(8,128)(2,1)} %get-tuple-element.7.refs_1_, bf16[2,72,1536]{2,1,0:T(8,128)(2,1)} %get-tuple-element.8.refs_2_), custom_call_target="tpu_custom_call" | custom-call | tf_op jit(solution)/shard_map/keep_results/pallas_call | solution.py:657
